TPU v7x, 256 devices: a whole 4x4x8 slice. The times are simulated.
256 devices in a mesh: ctx: 8 (over x, core), lang: 32 (over z, y).
Axes of the slice: x: 4, y: 4, z: 8, core: 2. Of those that a mesh axis runs over, the one named last changes fastest.
Arguments:
- attn_queries: bfloat16 [32, 1024, 1024], P('lang', 'ctx'), may hold values from -100 to 100
- attn_keys: bfloat16 [32, 1024, 1024], P('lang', 'ctx'), may hold values from -5 to 5
- attn_values: bfloat16 [32, 1024, 1024], P('lang', 'ctx'), may hold values from -6 to 6
- residual: bfloat16 [32, 1024, 1024], P('lang', 'ctx'), may hold values from -6 to 6
- cotangent: bfloat16 [32, 1024, 1024], P('lang', 'ctx'), may hold values from -6 to 6
- segment_ids: int32 [32, 1024], P('lang', 'ctx'), may hold values from 0 to 7, never falling along the last dimension, each value on 1 to 512 neighbouring positions
- language_ids: int32 [32, 1024, 1], P('lang', 'ctx'), may hold values from 0 to 31; in each aligned block of 128 rows (0 to 127, 128 to 255, ..., all dimensions but the last counted through in order) at most 5 rows name the same one
- token_counts: int32 [32], replicated, may hold values from 16 to 1023
- norm_gain: float32 [1024], replicated, may hold values from 0.1 to 1.9
- gate_weight: bfloat16 [32, 1024, 4096], P('lang', None, 'ctx'), may hold values from -0.1875 to 0.1875
- up_weight: bfloat16 [32, 1024, 4096], P('lang', None, 'ctx'), may hold values from -0.1875 to 0.1875
- down_weight: bfloat16 [32, 4096, 1024], P('lang', 'ctx'), may hold values from -0.09375 to 0.09375
Outputs:
- layer_out: bfloat16 [32, 1024, 1024], P('lang', 'ctx')
- grad_queries: bfloat16 [32, 1024, 1024], P('lang', 'ctx')
- grad_keys: bfloat16 [32, 1024, 1024], P('lang', 'ctx')
- grad_values: bfloat16 [32, 1024, 1024], P('lang', 'ctx')
- grad_residual: bfloat16 [32, 1024, 1024], P('lang', 'ctx')
- grad_gain: float32 [1024], replicated
- grad_gate: bfloat16 [32, 1024, 4096], P('lang', None, 'ctx')
- grad_up: bfloat16 [32, 1024, 4096], P('lang', None, 'ctx')
- grad_down: bfloat16 [32, 4096, 1024], P('lang', 'ctx')
Inputs may be any that keep to these rules, and one draw needn't show every extreme that they name: `language_ids`: in each aligned block of 128 positions (the positions of one device) no language is named by more than 5 positions, a bound that some block reaches. `segment_ids`: never falling along a sequence; each document holds 1 to 512 positions.
All inputs are finite; a program needn't handle non-finite values.
Results may differ from a plain program's by a relative error of at most 0.023.
Values may be sent and summed in bfloat16 or wider, within the bound.
A program may use at most 128 MiB of HBM per device.

v0:
```python
import functools

import jax
import jax.numpy as jnp
from jax import lax
from jax.experimental import pallas as pl
from jax.experimental.pallas import tpu as pltpu
from jax.sharding import PartitionSpec as P

HD = 128
EPSILON = 1e-06
CAP = 5
PITCH = 6
GROUPS = 2
MESH = pl.DeviceIdType.MESH
F32 = jnp.float32
BF16 = jnp.bfloat16
MASKED = -1e30


def dot_nn(a, b):
    return lax.dot_general(a, b, (((1,), (0,)), ((), ())), preferred_element_type=F32)


def dot_nt(a, b):
    return lax.dot_general(a, b, (((1,), (1,)), ((), ())), preferred_element_type=F32)


def at(start, size, step=None):
    return pl.ds(pl.multiple_of(start, step or size), size)


def kernel(
    nctx,
    nlang,
    q_hbm,
    k_hbm,
    v_hbm,
    residual,
    cotangent,
    segment,
    language,
    counts,
    gain,
    wg_hbm,
    wu_hbm,
    wd_hbm,
    layer_out,
    gq_hbm,
    gk_hbm,
    gv_hbm,
    grad_res,
    grad_gain,
    gwg_hbm,
    gwu_hbm,
    gwd_hbm,
    qh,
    kh,
    vh,
    segsend,
    segrow,
    segcol,
    probs_t,
    probs_h,
    attsend,
    att,
    wg,
    wu,
    wd,
    gwg,
    gwu,
    gwd,
    summed_s,
    normed_s,
    gout_s,
    gn_s,
    stack,
    sel,
    sel_t,
    spread,
    spread_t,
    stack_r,
    msg_s,
    msg_r,
    rows_n,
    rows_g,
    gh_s,
    hid_s,
    ggp_s,
    gup_s,
    part,
    pair_r,
    sum_s,
    mid_r,
    fin_r,
    grsend,
    grh,
    gqsend,
    gksend,
    gvsend,
    gain_s,
    gain_c,
    gain_l_s,
    gain_l,
    loc_sem,
    out_sem,
    in_s,
    in_r,
    att_ss,
    att_rs,
    lang_ss,
    lang_rs,
    near_ss,
    near_rs,
    half_ss,
    half_rs,
    sib_ss,
    sib_rs,
    pair_ss,
    pair_rs,
    mid_ss,
    mid_rs,
    fin_ss,
    fin_rs,
    gr_ss,
    gr_rs,
    go_ss,
    go_rs,
    gain_ss,
    gain_rs,
    gainl_ss,
    gainl_rs,
):
    T, D = residual.shape
    L = nctx * T
    J = D // HD
    X = nctx // 2
    assert X == 4
    F = wg.shape[1]
    H = D // 2
    MR = PITCH * J
    LG = nlang // GROUPS
    RG = LG * CAP
    OP = 128
    scale = HD ** (-0.5)
    c = lax.axis_index("ctx")
    me = lax.axis_index("lang")
    x = c // 2
    core = c % 2
    sib = x * 2 + 1 - core
    right, left, across = (x + 1) % X, (x + 3) % X, (x + 2) % X

    def rcopy(src, dst, ssem, rsem, dev):
        return pltpu.make_async_remote_copy(
            src_ref=src, dst_ref=dst, send_sem=ssem, recv_sem=rsem, device_id=dev, device_id_type=MESH
        )

    def loop(lo, hi, body):
        def step(i, carry):
            body(i)
            return carry

        lax.fori_loop(lo, hi, step, 0)

    scope = []

    def mark(name):
        if scope:
            scope.pop().__exit__(None, None, None)
        if name:
            scope.append(jax.named_scope(name))
            scope[-1].__enter__()

    mark("entry")
    weight_in = [
        pltpu.make_async_copy(src, dst, loc_sem.at[i])
        for i, (src, dst) in enumerate(((wd_hbm, wd), (wg_hbm, wg), (wu_hbm, wu)))
    ]
    own_in = [
        pltpu.make_async_copy(src.at[:, at(c * HD, HD)], dst.at[at(c * T, T)], loc_sem.at[3 + i])
        for i, (src, dst) in enumerate(((k_hbm, kh), (q_hbm, qh), (v_hbm, vh)))
    ]
    segsend[...] = jnp.broadcast_to(segment[...].astype(F32), segsend.shape).astype(BF16)

    barrier = pltpu.get_barrier_semaphore()
    loop(1, nctx, lambda i: pl.semaphore_signal(barrier, inc=1, device_id={"ctx": (c + i) % nctx}, device_id_type=MESH))
    loop(1, nlang, lambda i: pl.semaphore_signal(barrier, inc=1, device_id={"lang": (me + i) % nlang}, device_id_type=MESH))
    for copy in own_in:
        copy.start()
    pl.semaphore_wait(barrier, nctx - 1 + nlang - 1)

    mark("send_qkv")
    def in_copy(i, to, owner):
        if i == 3:
            src, dst = segsend, segrow.at[:, at(owner * T, T)]
        else:
            src, dst = ((k_hbm, kh), (q_hbm, qh), (v_hbm, vh))[i]
            src, dst = src.at[:, at(to * HD, HD)], dst.at[at(owner * T, T)]
        return rcopy(src, dst, in_s.at[i, to], in_r.at[i, owner], {"ctx": to})

    for which in ((3, 0), (1,), (2,)):

        def send_in(i):
            for n in which:
                in_copy(n, (c + i) % nctx, c).start()

        loop(1, nctx, send_in)
    for copy in weight_in:
        copy.start()
    segrow[:, at(c * T, T)] = segsend[...]

    mark("slots")
    lang_row = language[...].astype(F32)
    lang_col = jnp.transpose(jnp.broadcast_to(lang_row, (T, T)))
    earlier = lax.broadcasted_iota(jnp.int32, (T, T), 0) < lax.broadcasted_iota(jnp.int32, (T, T), 1)
    rank = jnp.sum(jnp.where((lang_col == lang_row) & earlier, 1.0, 0.0), axis=0, keepdims=True)
    slot_row = lang_row * float(MR) + rank
    slot_col = jnp.transpose(jnp.broadcast_to(slot_row, (T, T)))[:, 0:1].astype(jnp.int32)
    slot_row = slot_row.astype(jnp.int32)
    for j in range(J):
        hit = lax.broadcasted_iota(jnp.int32, (nlang * MR, T), 0) == slot_row + PITCH * j
        sel[:, j * T : (j + 1) * T] = jnp.where(hit, 1.0, 0.0).astype(BF16)

    lang_hit = lang_col[:, 0:1] == lax.broadcasted_iota(jnp.int32, (T, nlang), 1).astype(F32)
    count = jnp.sum(jnp.where(lang_hit, counts[...].astype(F32), 0.0), axis=1, keepdims=True)
    gout_s[...] = cotangent[...].astype(F32) * (16.0 * lax.rsqrt(count))

    NY = 4 if nlang % 8 == 0 else 1
    NZ = nlang // NY

    def partner(d, sign):
        if NY == 1:
            return (me + nlang + sign * d) % nlang
        turn_z = d // NY
        off_z = (2 * turn_z) % NZ + turn_z // (NZ // 2)
        return (me // NY + NZ + sign * off_z) % NZ * NY + (me % NY + NY + sign * (d % NY)) % NY

    def dispatch(phase, stacked):
        for j in range(J):
            stack[j * T : (j + 1) * T, :] = stacked[:, j * HD : (j + 1) * HD]
        msg_s[phase] = dot_nn(sel[...], stack[...]).astype(BF16)

        def one(d):
            to = partner(d, 1)
            rcopy(
                msg_s.at[phase, at(to * MR, MR)],
                msg_r.at[phase, at(d * MR, MR)],
                lang_ss.at[phase, d],
                lang_rs.at[phase, d],
                {"lang": to},
            ).start()

        loop(1, nlang, one)
        msg_r[phase, 0:MR, :] = msg_s[phase, at(me * MR, MR), :]

    def lang_wait(phase, lo, hi):
        def one(d):
            rcopy(
                msg_s.at[phase, at(d * MR, MR)],
                msg_r.at[phase, at(d * MR, MR)],
                lang_ss.at[phase, d],
                lang_rs.at[phase, d],
                {"lang": me},
            ).wait_recv()

        loop(lo, hi, one)

    def lang_wait_but_own(phase):
        def one(d):
            l = (me + d) % nlang
            rcopy(
                msg_s.at[phase, at(l * MR, MR)],
                msg_r.at[phase, at(l * MR, MR)],
                lang_ss.at[phase, d],
                lang_rs.at[phase, l],
                {"lang": me},
            ).wait_recv()

        loop(1, nlang, one)

    mark("dispatch_grads")
    dispatch(0, gout_s[...].astype(BF16))

    mark("spread")
    o_col = lax.broadcasted_iota(jnp.int32, (RG, LG * MR), 0)
    base = ((o_col * 205) >> 10) * (MR - CAP) + o_col
    for j in range(J):
        hit = lax.broadcasted_iota(jnp.int32, (RG, LG * MR), 1) == base + PITCH * j
        spread[j * RG : (j + 1) * RG, :] = jnp.where(hit, 1.0, 0.0).astype(BF16)

    mark("wait_qkv")
    for copy in own_in:
        copy.wait()

    def wait_in(n):
        loop(1, nctx, lambda i: in_copy(n, (c + i) % nctx, (c + i) % nctx).wait_recv())

    for n in (3, 0, 1):
        wait_in(n)
    for p in range(nctx):
        row = segrow[0:1, p * T : (p + 1) * T].astype(F32)
        segcol[p * T : (p + 1) * T, :] = jnp.transpose(jnp.broadcast_to(row, (T, T)))

    mark("attention")
    def forward(i):
        p = (c + 1 + i) % nctx
        s = dot_nt(qh[at(p * T, T), :], kh[...]) * scale
        same = segcol[at(p * T, T), 0:1] == segrow[0:1, :].astype(F32)
        s = jnp.where(same, s, MASKED)
        e = jnp.exp(s - jnp.max(s, axis=1, keepdims=True))
        probs_h[at(i * T, T), :] = (e / jnp.sum(e, axis=1, keepdims=True)).astype(BF16)

    loop(0, nctx, forward)
    mark("wait_values")
    wait_in(2)
    mark("attended")

    def attend(i):
        p = (c + 1 + i) % nctx
        attsend[at(p * T, T), :] = dot_nn(probs_h[at(i * T, T), :], vh[...]).astype(BF16)

        @pl.when(i < nctx - 1)
        def _():
            rcopy(attsend.at[at(p * T, T)], att.at[:, at(c * HD, HD)], att_ss.at[p], att_rs.at[c], {"ctx": p}).start()

    loop(0, nctx, attend)
    att[:, at(c * HD, HD)] = attsend[at(c * T, T), :]

    def block(chip, g, k):
        return at(((chip * GROUPS + g) * 2 + k) * RG, RG, 16)

    def near_copy(w, buf, g, side):
        rows = block(x, g, core)
        to = (right, left)[side] * 2 + core
        n = w * GROUPS + g
        return rcopy(buf.at[rows], buf.at[rows], near_ss.at[n, side], near_rs.at[n, side], {"ctx": to})

    def half_copy(w, buf, g, side):
        rows = block((left, right)[side], g, core)
        cols = slice(side * H, (side + 1) * H)
        to = (right, left)[side] * 2 + core
        n = w * GROUPS + g
        return rcopy(buf.at[rows, cols], buf.at[rows, cols], half_ss.at[n, side], half_rs.at[n, side], {"ctx": to})

    def sib_copy(w, buf, g, what, k=core):
        n = w * GROUPS + g
        rows = block((x, left, right, across, across)[what], g, k)
        cols = slice(None) if what < 3 else slice((what - 3) * H, (what - 2) * H)
        return rcopy(buf.at[rows, cols], buf.at[rows, cols], sib_ss.at[n, what], sib_rs.at[n, what], {"ctx": sib})

    def gather_send(w, buf, phase, g):
        lang_wait(phase, max(1, g * LG), (g + 1) * LG)
        rows = block(x, g, core)
        for j in range(J):
            buf[rows, j * HD : (j + 1) * HD] = dot_nn(
                spread[j * RG : (j + 1) * RG, :], msg_r[phase, g * LG * MR : (g + 1) * LG * MR, :]
            ).astype(BF16)
        near_copy(w, buf, g, 0).start()
        near_copy(w, buf, g, 1).start()
        sib_copy(w, buf, g, 0).start()

    def near_forward(w, buf, g):
        for side in range(2):
            rows = block((left, right)[side], g, core)
            n = w * GROUPS + g
            rcopy(buf.at[rows], buf.at[rows], near_ss.at[n, side], near_rs.at[n, side], {"ctx": sib}).wait_recv()
            half_copy(w, buf, g, side).start()
            sib_copy(w, buf, g, 1 + side).start()

    def half_forward(w, buf, g):
        for side in range(2):
            rows = block(across, g, core)
            cols = slice(side * H, (side + 1) * H)
            n = w * GROUPS + g
            rcopy(
                buf.at[rows, cols], buf.at[rows, cols], half_ss.at[n, side], half_rs.at[n, side], {"ctx": sib}
            ).wait_recv()
            sib_copy(w, buf, g, 3 + side).start()

    def sib_wait(w, buf, g, what):
        sib_copy(w, buf, g, what, 1 - core).wait_recv()

    mark("grad_rows")
    for g in range(GROUPS):
        gather_send(0, rows_g, 0, g)

    mark("wait_attended")
    def wait_att(i):
        p = (c + i) % nctx
        rcopy(attsend.at[at(p * T, T)], att.at[:, at(p * HD, HD)], att_ss.at[p], att_rs.at[p], {"ctx": p}).wait_recv()

    loop(1, nctx, wait_att)
    mark("norm_dispatch")
    summed = residual[...].astype(F32) + att[...].astype(F32)
    summed_s[...] = summed
    inv_rms = lax.rsqrt(jnp.mean(summed * summed, axis=1, keepdims=True) + EPSILON)
    normed = summed * inv_rms
    normed_s[...] = normed
    dispatch(1, (normed * gain[...]).astype(BF16))

    mark("layouts")
    for j in range(J):
        hit = lax.broadcasted_iota(jnp.int32, (T, nlang * MR), 1) == slot_col + PITCH * j
        sel_t[j * T : (j + 1) * T, :] = jnp.where(hit, 1.0, 0.0).astype(BF16)
    o_row = lax.broadcasted_iota(jnp.int32, (LG * MR, OP), 1)
    base_row = ((o_row * 205) >> 10) * (MR - CAP) + o_row
    inside = o_row < RG
    for j in range(J):
        hit = (lax.broadcasted_iota(jnp.int32, (LG * MR, OP), 0) == base_row + PITCH * j) & inside
        spread_t[:, j * OP : (j + 1) * OP] = jnp.where(hit, 1.0, 0.0).astype(BF16)
    stack_r[...] = jnp.zeros_like(stack_r)

    mark("back_probs")

    def back_probs(p):
        s = dot_nt(kh[...], qh[at(p * T, T), :]) * scale
        same = segcol[...] == segrow[0:1, at(p * T, T)].astype(F32)
        s = jnp.where(same, s, MASKED)
        e = jnp.exp(s - jnp.max(s, axis=0, keepdims=True))
        probs = e / jnp.sum(e, axis=0, keepdims=True)
        probs_t[at(p * L, L), :] = probs
        probs_h[:, at(p * T, T)] = probs.astype(BF16)

    loop(0, nctx, back_probs)
    mark("forward_grads")
    for g in range(GROUPS):
        near_forward(0, rows_g, g)
    mark("norm_rows")
    for g in range(GROUPS):
        gather_send(1, rows_n, 1, g)
        half_forward(0, rows_g, g)
    mark("grad_hidden")
    weight_in[0].wait()
    CR = GROUPS * 2 * RG
    for g in range(GROUPS):
        for what in range(5):
            sib_wait(0, rows_g, g, what)

    def grad_hidden(i):
        rows = at(i * CR, CR, 16)
        gh_s[rows, :] = dot_nt(rows_g[rows, :], wd[...])

    loop(0, X, grad_hidden)
    weight_in[1].wait()
    weight_in[2].wait()

    FT = min(F, 256)
    DT = min(D, 512)

    def flat(chip, g):
        return at((chip * GROUPS + g) * RG, RG, 16)

    def pair_copy(w, chip, g):
        n = chip * GROUPS + g
        return rcopy(
            part.at[w, block(chip, g, 1 - core)], pair_r.at[w, flat(chip, g)], pair_ss.at[w, n], pair_rs.at[w, n], {"ctx": sib}
        )

    def pair_sum(w, chip, g, cols):
        own = part[w, block(chip, g, core), cols].astype(F32)
        return own + pair_r[w, flat(chip, g), cols].astype(F32)

    halves = (slice(0, H), slice(H, D))

    def mid_copy(w, g, h):
        to = (right, left)[h] * 2 + core
        src = sum_s.at[w, flat(across, g), halves[h]]
        n = w * GROUPS + g
        return rcopy(src, mid_r.at[w, at(g * RG, RG, 16), halves[h]], mid_ss.at[n, h], mid_rs.at[n, h], {"ctx": to})

    def fin_copy(w, g, side, h):
        chip = (right, left)[side]
        src = sum_s.at[w, flat(chip, g), halves[h]]
        dst = fin_r.at[w, at((side * GROUPS + g) * RG, RG, 16), halves[h]]
        n = w * GROUPS + g
        return rcopy(src, dst, fin_ss.at[n, side * 2 + h], fin_rs.at[n, side * 2 + h], {"ctx": chip * 2 + core})

    def sum_across(w, g):
        pair_copy(w, across, g).wait_recv()
        for h in range(2):
            sum_s[w, flat(across, g), halves[h]] = pair_sum(w, across, g, halves[h]).astype(BF16)
            mid_copy(w, g, h).start()

    def sum_near(w, g, side):
        chip, h = (right, left)[side], 1 - side
        pair_copy(w, chip, g).wait_recv()
        sum_s[w, flat(chip, g), halves[h]] = pair_sum(w, chip, g, halves[h]).astype(BF16)
        fin_copy(w, g, side, h).start()

    def sum_late(w, g):
        for side in range(2):
            chip, h = (right, left)[side], side
            mid_copy(w, g, h).wait_recv()
            total = pair_sum(w, chip, g, halves[h]) + mid_r[w, at(g * RG, RG, 16), halves[h]].astype(F32)
            sum_s[w, flat(chip, g), halves[h]] = total.astype(BF16)
            fin_copy(w, g, side, h).start()

    def sum_own(w, g):
        pair_copy(w, x, g).wait_recv()
        for side in range(2):
            for h in range(2):
                fin_copy(w, g, side, h).wait_recv()
        total = pair_sum(w, x, g, slice(None))
        for side in range(2):
            total = total + fin_r[w, at((side * GROUPS + g) * RG, RG, 16), :].astype(F32)
        return total.astype(BF16)

    def feed(rows):
        for n in range(F // FT):
            cols = slice(n * FT, (n + 1) * FT)
            pre_gate = dot_nn(rows_n[rows, :], wg[:, cols])
            pre_up = dot_nn(rows_n[rows, :], wu[:, cols])
            gh = gh_s[rows, cols]
            sig = jax.nn.sigmoid(pre_gate)
            silu = pre_gate * sig
            hid_s[rows, cols] = (silu * pre_up).astype(BF16)
            ggp_s[rows, cols] = (gh * pre_up * sig * (1.0 + pre_gate * (1.0 - sig))).astype(BF16)
            gup_s[rows, cols] = (gh * silu).astype(BF16)
        for n in range(D // DT):
            cols = slice(n * DT, (n + 1) * DT)
            part[0, rows, cols] = (dot_nt(ggp_s[rows, :], wg[cols, :]) + dot_nt(gup_s[rows, :], wu[cols, :])).astype(BF16)

    def feed_chip(i):
        chip = (x + i + i // 2) % X
        for g in range(GROUPS):
            for what, when in ((0, 0), (2, 1), (1, 2)):

                @pl.when(i == when)
                def _():
                    sib_wait(1, rows_n, g, what)

        feed(at(chip * CR, CR, 16))
        for g in range(GROUPS):
            pair_copy(0, chip, g).start()

    mark("feed_own")
    loop(0, 1, feed_chip)
    mark("feed_near_wait")
    for g in range(GROUPS):
        near_forward(1, rows_n, g)
    mark("feed_near")
    loop(1, 3, feed_chip)
    mark("sum_near")
    for g in range(GROUPS):
        for side in range(2):
            sum_near(0, g, side)
    for g in range(GROUPS):
        half_forward(1, rows_n, g)
    mark("feed_across")

    def feed_across(g):
        for m in range(GROUPS):

            @pl.when(g == m)
            def _():
                sib_wait(1, rows_n, m, 3)
                sib_wait(1, rows_n, m, 4)

        feed(at((across * GROUPS + g) * 2 * RG, 2 * RG, 16))
        pair_copy(0, across, g).start()

    loop(0, GROUPS, feed_across)
    mark("sum_across")
    for g in range(GROUPS):
        sum_across(0, g)

    mark("down")

    def down(i):
        rows = at(i * CR, CR, 16)
        part[1, rows, :] = dot_nn(hid_s[rows, :], wd[...]).astype(BF16)
        for g in range(GROUPS):
            pair_copy(1, i, g).start()

    loop(0, X, down)
    mark("sum_late")
    for g in range(GROUPS):
        sum_late(0, g)

    def grad_w(n):
        cols = at(n * FT, FT)
        turned = jnp.transpose(rows_n[:, cols])
        gwg[cols, :] = dot_nn(turned, ggp_s[...]).astype(BF16)
        gwu[cols, :] = dot_nn(turned, gup_s[...]).astype(BF16)

    def grad_wd(n):
        cols = at(n * FT, FT)
        gwd[cols, :] = dot_nn(jnp.transpose(hid_s[:, cols]), rows_g[...]).astype(BF16)

    def return_send(w, phase):
        for g in range(GROUPS):
            total = sum_own(w, g)
            for j in range(J):
                stack_r[j * OP : j * OP + RG, :] = total[:, j * HD : (j + 1) * HD]
            msg_s[phase, g * LG * MR : (g + 1) * LG * MR, :] = dot_nn(spread_t[...], stack_r[...]).astype(BF16)

            def one(d):
                to = partner(d, -1)
                rcopy(
                    msg_s.at[phase, at(d * MR, MR)],
                    msg_r.at[phase, at(me * MR, MR)],
                    lang_ss.at[phase, d],
                    lang_rs.at[phase, me],
                    {"lang": to},
                ).start()

            loop(max(1, g * LG), (g + 1) * LG, one)
        msg_r[phase, at(me * MR, MR), :] = msg_s[phase, 0:MR, :]

    def combine(phase):
        lang_wait_but_own(phase)
        for j in range(J):
            gn_s[:, j * HD : (j + 1) * HD] = dot_nn(sel_t[j * T : (j + 1) * T, :], msg_r[phase])

    mark("grad_w_a")
    half = max(1, (D // FT) // 2)
    loop(0, half, grad_w)
    mark("return_grads")
    return_send(0, 2)
    mark("ffn_sums")
    for g in range(GROUPS):
        sum_across(1, g)
    for g in range(GROUPS):
        for side in range(2):
            sum_near(1, g, side)
    mark("grad_w_b")
    loop(half, D // FT, grad_w)
    mark("ffn_late")
    for g in range(GROUPS):
        sum_late(1, g)
    mark("grad_wd")
    out_w = [
        pltpu.make_async_copy(src, dst, out_sem.at[i])
        for i, (src, dst) in enumerate(((gwg, gwg_hbm), (gwu, gwu_hbm), (gwd, gwd_hbm)))
    ]
    out_w[0].start()
    out_w[1].start()
    loop(0, F // FT, grad_wd)
    out_w[2].start()

    mark("combine_grads")
    combine(2)
    mark("grad_residual")
    grad_normin = gn_s[...]
    normed = normed_s[...]
    summed = summed_s[...]
    inv_rms = lax.rsqrt(jnp.mean(summed * summed, axis=1, keepdims=True) + EPSILON)
    scaled = grad_normin * gain[...]
    gres = gout_s[...] + inv_rms * (scaled - normed * jnp.mean(scaled * normed, axis=1, keepdims=True))
    grsend[...] = gres.astype(BF16)

    def gr_copy(to, owner, sem_at):
        return rcopy(grsend.at[:, at(to * HD, HD)], grh.at[at(owner * T, T)], gr_ss.at[sem_at], gr_rs.at[owner], {"ctx": to})

    loop(1, nctx, lambda i: gr_copy((c + i) % nctx, c, (c + i) % nctx).start())
    grh[at(c * T, T), :] = grsend[:, at(c * HD, HD)]
    grad_res[...] = grsend[...]
    gain_part = jnp.sum(grad_normin * normed, axis=0, keepdims=True)
    for j in range(J):
        gain_s[j : j + 1, :] = gain_part[:, j * HD : (j + 1) * HD]

    def gain_copy(to, owner):
        return rcopy(gain_s, gain_c.at[owner], gain_ss.at[to], gain_rs.at[owner], {"ctx": to})

    loop(1, nctx, lambda i: gain_copy((c + i) % nctx, c).start())
    gain_c[c] = gain_s[...]

    mark("return_ffn")
    return_send(1, 3)

    mark("backward")
    def go_copy(n, src, dst, to, owner):
        return rcopy(src.at[at(to * T, T)], dst.at[:, at(owner * HD, HD)], go_ss.at[n, to], go_rs.at[n, owner], {"ctx": to})

    loop(1, nctx, lambda i: gr_copy((c + i) % nctx, (c + i) % nctx, (c + i) % nctx).wait_recv())
    mark("grad_values")
    gvsend[...] = dot_nn(probs_h[...], grh[...]).astype(BF16)
    loop(1, nctx, lambda i: go_copy(2, gvsend, gv_hbm, (c + i) % nctx, c).start())
    mark("gain")

    loop(1, nctx, lambda i: gain_copy((c + i) % nctx, (c + i) % nctx).wait_recv())
    gain_l_s[...] = jnp.sum(gain_c[...], axis=0)

    def gainl_copy(to, owner):
        return rcopy(gain_l_s, gain_l.at[owner], gainl_ss.at[to], gainl_rs.at[owner], {"lang": to})

    loop(1, nlang, lambda i: gainl_copy((me + i) % nlang, me).start())
    gain_l[me] = gain_l_s[...]
    mark("backward_loop")

    def backward(i):
        p = (c + 1 + i) % nctx
        probs = probs_t[at(p * L, L), :]
        gp = dot_nt(vh[...], grh[at(p * T, T), :])
        gs = (probs * (gp - jnp.sum(probs * gp, axis=0, keepdims=True))).astype(BF16)
        probs_h[:, at(p * T, T)] = gs
        gqsend[at(p * T, T), :] = (dot_nn(jnp.transpose(gs), kh[...]) * scale).astype(BF16)

        @pl.when(i < nctx - 1)
        def _():
            go_copy(0, gqsend, gq_hbm, p, c).start()

    loop(0, nctx, backward)
    mark("send_keys")
    gksend[...] = (dot_nn(probs_h[...], qh[...]) * scale).astype(BF16)
    loop(1, nctx, lambda i: go_copy(1, gksend, gk_hbm, (c + i) % nctx, c).start())
    triples = ((gqsend, gq_hbm), (gksend, gk_hbm), (gvsend, gv_hbm))
    own_out = [
        pltpu.make_async_copy(src.at[at(c * T, T)], dst.at[:, at(c * HD, HD)], loc_sem.at[3 + n])
        for n, (src, dst) in enumerate(triples)
    ]
    for copy in own_out:
        copy.start()

    mark("combine_ffn")
    combine(3)
    layer_out[...] = (summed_s[...] + gn_s[...]).astype(BF16)

    mark("gain_wait")
    loop(1, nlang, lambda i: gainl_copy((me + i) % nlang, (me + i) % nlang).wait_recv())
    grad_gain[...] = jnp.sum(gain_l[...], axis=0)

    mark("wait_out")
    def wait_out(i):
        p = (c + i) % nctx
        for n, (src, dst) in enumerate(triples):
            go_copy(n, src, dst, p, p).wait_recv()

    loop(1, nctx, wait_out)

    mark("wait_sent")
    def sent_ctx(i):
        p = (c + i) % nctx
        for n in range(4):
            in_copy(n, p, c).wait_send()
        rcopy(attsend.at[at(p * T, T)], att.at[:, at(c * HD, HD)], att_ss.at[p], att_rs.at[c], {"ctx": p}).wait_send()
        gr_copy(p, c, p).wait_send()
        gain_copy(p, c).wait_send()
        for n, (src, dst) in enumerate(triples):
            go_copy(n, src, dst, p, c).wait_send()

    loop(1, nctx, sent_ctx)

    def sent_lang(d):
        for phase in range(4):
            rcopy(
                msg_s.at[phase, at(d * MR, MR)],
                msg_r.at[phase, at(d * MR, MR)],
                lang_ss.at[phase, d],
                lang_rs.at[phase, d],
                {"lang": (me + d) % nlang},
            ).wait_send()
        gainl_copy((me + d) % nlang, me).wait_send()

    loop(1, nlang, sent_lang)

    for w, buf in ((0, rows_g), (1, rows_n)):
        for g in range(GROUPS):
            for side in range(2):
                near_copy(w, buf, g, side).wait_send()
                half_copy(w, buf, g, side).wait_send()
                mid_copy(w, g, side).wait_send()
                for h in range(2):
                    fin_copy(w, g, side, h).wait_send()
            for what in range(5):
                sib_copy(w, buf, g, what).wait_send()

    def sent_pair(i):
        for w in range(2):
            for g in range(GROUPS):
                pair_copy(w, i, g).wait_send()

    loop(0, X, sent_pair)
    for copy in own_out:
        copy.wait()
    for copy in out_w:
        copy.wait()
    mark(None)


def store(*refs):
    n = (len(refs) - 2) // 3
    fetch_sem, store_sem = refs[-2:]
    fetches = [pltpu.make_async_copy(refs[i], refs[2 * n + i], fetch_sem.at[i]) for i in range(n)]
    stores = [pltpu.make_async_copy(refs[2 * n + i], refs[n + i], store_sem.at[i]) for i in range(n)]
    for copy in fetches:
        copy.start()
    for fetch, copy in zip(fetches, stores):
        fetch.wait()
        copy.start()
    for copy in stores:
        copy.wait()


def local(
    attn_queries,
    attn_keys,
    attn_values,
    residual,
    cotangent,
    segment_ids,
    language_ids,
    token_counts,
    norm_gain,
    gate_weight,
    up_weight,
    down_weight,
):
    nctx = lax.axis_size("ctx")
    nlang = lax.axis_size("lang")
    T, D = attn_queries.shape[1:]
    F = gate_weight.shape[2]
    L = nctx * T
    J = D // HD
    X = nctx // 2
    MR = PITCH * J
    LG = nlang // GROUPS
    RG = LG * CAP
    BR = nlang * CAP
    R = nctx * BR
    vmem = lambda *shape: pltpu.VMEM(shape, BF16)
    vmem32 = lambda *shape: pltpu.VMEM(shape, F32)
    dma = lambda *shape: pltpu.SemaphoreType.DMA(shape)
    scratch = [
        vmem(L, HD),
        vmem(L, HD),
        vmem(L, HD),
        vmem(16, T),
        vmem(16, L),
        vmem32(L, T),
        vmem32(nctx * L, T),
        vmem(L, L),
        vmem(L, HD),
        vmem(T, D),
        vmem(D, F),
        vmem(D, F),
        vmem(F, D),
        vmem(D, F),
        vmem(D, F),
        vmem(F, D),
        vmem32(T, D),
        vmem32(T, D),
        vmem32(T, D),
        vmem32(T, D),
        vmem(J * T, HD),
        vmem(nlang * MR, J * T),
        vmem(J * T, nlang * MR),
        vmem(J * RG, LG * MR),
        vmem(LG * MR, J * 128),
        vmem(J * 128, HD),
        vmem(4, nlang * MR, HD),
        vmem(4, nlang * MR, HD),
        vmem(R, D),
        vmem(R, D),
        vmem32(R, F),
        vmem(R, F),
        vmem(R, F),
        vmem(R, F),
        vmem(2, R, D),
        vmem(2, X * BR, D),
        vmem(2, X * BR, D),
        vmem(2, BR, D),
        vmem(2, 2 * BR, D),
        vmem(T, D),
        vmem(L, HD),
        vmem(L, HD),
        vmem(L, HD),
        vmem(L, HD),
        vmem32(J, HD),
        vmem32(nctx, J, HD),
        vmem32(J, HD),
        vmem32(nlang, J, HD),
        dma(6),
        dma(3),
        dma(4, nctx),
        dma(4, nctx),
        dma(nctx),
        dma(nctx),
        dma(4, nlang),
        dma(4, nlang),
        dma(2 * GROUPS, 2),
        dma(2 * GROUPS, 2),
        dma(2 * GROUPS, 2),
        dma(2 * GROUPS, 2),
        dma(2 * GROUPS, 5),
        dma(2 * GROUPS, 5),
        dma(2, X * GROUPS),
        dma(2, X * GROUPS),
        dma(2 * GROUPS, 2),
        dma(2 * GROUPS, 2),
        dma(2 * GROUPS, 4),
        dma(2 * GROUPS, 4),
        dma(nctx),
        dma(nctx),
        dma(3, nctx),
        dma(3, nctx),
        dma(nctx),
        dma(nctx),
        dma(nlang),
        dma(nlang),
    ]
    anywhere = pl.BlockSpec(memory_space=pl.ANY)
    inside = pl.BlockSpec(memory_space=pltpu.VMEM)
    shape = lambda *dims: jax.ShapeDtypeStruct(dims, BF16)
    outs = pl.pallas_call(
        functools.partial(kernel, nctx, nlang),
        out_shape=(
            shape(T, D),
            shape(T, D),
            shape(T, D),
            shape(T, D),
            shape(T, D),
            jax.ShapeDtypeStruct((J, HD), F32),
            shape(D, F),
            shape(D, F),
            shape(F, D),
        ),
        in_specs=[anywhere] * 3 + [inside] * 6 + [anywhere] * 3,
        out_specs=(inside, anywhere, anywhere, anywhere, inside, inside, anywhere, anywhere, anywhere),
        scratch_shapes=scratch,
        compiler_params=pltpu.CompilerParams(collective_id=0, has_side_effects=True, vmem_limit_bytes=58 * 1024 * 1024),
        cost_estimate=pl.CostEstimate(flops=16_000_000_000, bytes_accessed=10_000_000, transcendentals=3_000_000),
        name="layer",
    )(
        attn_queries[0],
        attn_keys[0],
        attn_values[0],
        residual[0],
        cotangent[0],
        segment_ids,
        language_ids.reshape(1, T),
        token_counts.reshape(1, nlang),
        norm_gain.reshape(1, D),
        gate_weight[0],
        up_weight[0],
        down_weight[0],
    )
    outs = pl.pallas_call(
        store,
        out_shape=tuple(jax.ShapeDtypeStruct(o.shape, o.dtype) for o in outs),
        in_specs=[anywhere] * len(outs),
        out_specs=(anywhere,) * len(outs),
        scratch_shapes=[pltpu.VMEM(o.shape, o.dtype) for o in outs] + [dma(len(outs)), dma(len(outs))],
        compiler_params=pltpu.CompilerParams(vmem_limit_bytes=58 * 1024 * 1024),
        name="store",
    )(*outs)
    layer_out, gq, gk, gv, gres, ggain, gwg, gwu, gwd = outs
    return (
        layer_out[None],
        gq[None],
        gk[None],
        gv[None],
        gres[None],
        ggain.reshape(D),
        gwg[None],
        gwu[None],
        gwd[None],
    )


def solution(mesh):
    block = P("lang", "ctx", None)
    in_specs = (
        block,
        block,
        block,
        block,
        block,
        P("lang", "ctx"),
        block,
        P(),
        P(),
        P("lang", None, "ctx"),
        P("lang", None, "ctx"),
        block,
    )
    out_specs = (
        block,
        block,
        block,
        block,
        block,
        P(),
        P("lang", None, "ctx"),
        P("lang", None, "ctx"),
        block,
    )
    return jax.shard_map(local, mesh=mesh, in_specs=in_specs, out_specs=out_specs, check_vma=False)
```

profile of v0, /device:TPU:1, one launch (start us, length us, event | category | flops | bytes accessed | tf_op | source)
XLA Modules:
  0.0 116.7 jit_solution(14256407550095295177)
XLA Ops:
  0.6 111.5 %layer.1 = (bf16[128,1024]{1,0:T(8,128)(2,1)}, bf16[128,1024]{1,0:T(8,128)(2,1)}, bf16[128,1024]{1,0:T(8,128)(2,1)}, bf16[128,1024]{1,0:T(8,128)(2,1)}, bf16[128...) custom-call(bf16[128,1024]{1,0:T(8,128)(2,1)} %bitcast.26, ...), custom_call_target="tpu_custom_call" | custom-call | flops 16000000000 | bytes 10000000 | tf_op jit(solution)/shard_map/layer/pallas_call | solution.py:905
  112.2 4.3 %store.1 = (bf16[128,1024]{1,0:T(8,128)(2,1)}, bf16[128,1024]{1,0:T(8,128)(2,1)}, bf16[128,1024]{1,0:T(8,128)(2,1)}, bf16[128,1024]{1,0:T(8,128)(2,1)}, bf16[128...) custom-call(bf16[128,1024]{1,0:T(8,128)(2,1)} %get-tuple-element.27., ...), custom_call_target="tpu_custom_call" | custom-call | tf_op jit(solution)/shard_map/store/pallas_call | solution.py:938
where the time goes:
time: 117 us
  Pallas kernels  116 us (99%)
    pallas_call x1, Pallas kernels, local(): pl.pallas_call(functools.partial(kernel, nctx, nlang), out_shape=(shape(T...  112 us
    pallas_call x1, Pallas kernels, local(): pl.pallas_call(store, out_shape=tuple((jax.ShapeDtypeStruct(o.shape, o.dt...  4.3 us

commit v1 on v0

--- a/solution.py
+++ b/solution.py
@@ -62,6 +62,7 @@
     segcol,
     probs_t,
     probs_h,
+    kh_t,
     attsend,
     att,
     wg,
@@ -155,12 +156,16 @@
             src_ref=src, dst_ref=dst, send_sem=ssem, recv_sem=rsem, device_id=dev, device_id_type=MESH
         )
 
-    def loop(lo, hi, body):
+    def each(lo, hi, body):
+        for i in range(lo, hi):
+            body(i)
+
+    def loop(lo, hi, body, unroll=1):
         def step(i, carry):
             body(i)
             return carry
 
-        lax.fori_loop(lo, hi, step, 0)
+        lax.fori_loop(lo, hi, step, 0, unroll=unroll)
 
     scope = []
 
@@ -183,8 +188,8 @@
     segsend[...] = jnp.broadcast_to(segment[...].astype(F32), segsend.shape).astype(BF16)
 
     barrier = pltpu.get_barrier_semaphore()
-    loop(1, nctx, lambda i: pl.semaphore_signal(barrier, inc=1, device_id={"ctx": (c + i) % nctx}, device_id_type=MESH))
-    loop(1, nlang, lambda i: pl.semaphore_signal(barrier, inc=1, device_id={"lang": (me + i) % nlang}, device_id_type=MESH))
+    loop(1, nctx, lambda i: pl.semaphore_signal(barrier, inc=1, device_id={"ctx": lax.rem(c + i, nctx)}, device_id_type=MESH))
+    loop(1, nlang, lambda i: pl.semaphore_signal(barrier, inc=1, device_id={"lang": lax.rem(me + i, nlang)}, device_id_type=MESH))
     for copy in own_in:
         copy.start()
     pl.semaphore_wait(barrier, nctx - 1 + nlang - 1)
@@ -202,9 +207,9 @@
 
         def send_in(i):
             for n in which:
-                in_copy(n, (c + i) % nctx, c).start()
-
-        loop(1, nctx, send_in)
+                in_copy(n, lax.rem(c + i, nctx), c).start()
+
+        each(1, nctx, send_in)
     for copy in weight_in:
         copy.start()
     segrow[:, at(c * T, T)] = segsend[...]
@@ -227,13 +232,14 @@
 
     NY = 4 if nlang % 8 == 0 else 1
     NZ = nlang // NY
+    me_z, me_y = lax.div(me, NY), lax.rem(me, NY)
 
     def partner(d, sign):
         if NY == 1:
-            return (me + nlang + sign * d) % nlang
+            return lax.rem(me + nlang + sign * d, nlang)
         turn_z = d // NY
         off_z = (2 * turn_z) % NZ + turn_z // (NZ // 2)
-        return (me // NY + NZ + sign * off_z) % NZ * NY + (me % NY + NY + sign * (d % NY)) % NY
+        return lax.rem(me_z + NZ + sign * off_z, NZ) * NY + lax.rem(me_y + NY + sign * (d % NY), NY)
 
     def dispatch(phase, stacked):
         for j in range(J):
@@ -250,7 +256,7 @@
                 {"lang": to},
             ).start()
 
-        loop(1, nlang, one)
+        each(1, nlang, one)
         msg_r[phase, 0:MR, :] = msg_s[phase, at(me * MR, MR), :]
 
     def lang_wait(phase, lo, hi):
@@ -263,11 +269,11 @@
                 {"lang": me},
             ).wait_recv()
 
-        loop(lo, hi, one)
+        each(lo, hi, one)
 
     def lang_wait_but_own(phase):
         def one(d):
-            l = (me + d) % nlang
+            l = lax.rem(me + d, nlang)
             rcopy(
                 msg_s.at[phase, at(l * MR, MR)],
                 msg_r.at[phase, at(l * MR, MR)],
@@ -276,7 +282,7 @@
                 {"lang": me},
             ).wait_recv()
 
-        loop(1, nlang, one)
+        each(1, nlang, one)
 
     mark("dispatch_grads")
     dispatch(0, gout_s[...].astype(BF16))
@@ -293,9 +299,9 @@
         copy.wait()
 
     def wait_in(n):
-        loop(1, nctx, lambda i: in_copy(n, (c + i) % nctx, (c + i) % nctx).wait_recv())
-
-    for n in (3, 0, 1):
+        each(1, nctx, lambda i: in_copy(n, lax.rem(c + i, nctx), lax.rem(c + i, nctx)).wait_recv())
+
+    for n in (3, 0):
         wait_in(n)
     for p in range(nctx):
         row = segrow[0:1, p * T : (p + 1) * T].astype(F32)
@@ -303,27 +309,32 @@
 
     mark("attention")
     def forward(i):
-        p = (c + 1 + i) % nctx
+        p = lax.rem(c + nctx - i, nctx)
         s = dot_nt(qh[at(p * T, T), :], kh[...]) * scale
         same = segcol[at(p * T, T), 0:1] == segrow[0:1, :].astype(F32)
         s = jnp.where(same, s, MASKED)
         e = jnp.exp(s - jnp.max(s, axis=1, keepdims=True))
-        probs_h[at(i * T, T), :] = (e / jnp.sum(e, axis=1, keepdims=True)).astype(BF16)
-
-    loop(0, nctx, forward)
+        probs_h[at(p * T, T), :] = (e / jnp.sum(e, axis=1, keepdims=True)).astype(BF16)
+
+    def wait_query(i):
+        p = lax.rem(c + nctx - i, nctx)
+        in_copy(1, p, p).wait_recv()
+
+    BATCH = nctx // 2
+    for first in range(0, nctx, BATCH):
+        each(max(1, first), first + BATCH, wait_query)
+        loop(first, first + BATCH, forward, BATCH)
     mark("wait_values")
     wait_in(2)
     mark("attended")
 
-    def attend(i):
-        p = (c + 1 + i) % nctx
-        attsend[at(p * T, T), :] = dot_nn(probs_h[at(i * T, T), :], vh[...]).astype(BF16)
-
-        @pl.when(i < nctx - 1)
-        def _():
-            rcopy(attsend.at[at(p * T, T)], att.at[:, at(c * HD, HD)], att_ss.at[p], att_rs.at[c], {"ctx": p}).start()
-
-    loop(0, nctx, attend)
+    attsend[...] = dot_nn(probs_h[...], vh[...]).astype(BF16)
+
+    def send_attended(i):
+        p = lax.rem(c + i, nctx)
+        rcopy(attsend.at[at(p * T, T)], att.at[:, at(c * HD, HD)], att_ss.at[p], att_rs.at[c], {"ctx": p}).start()
+
+    each(1, nctx, send_attended)
     att[:, at(c * HD, HD)] = attsend[at(c * T, T), :]
 
     def block(chip, g, k):
@@ -386,10 +397,10 @@
 
     mark("wait_attended")
     def wait_att(i):
-        p = (c + i) % nctx
+        p = lax.rem(c + i, nctx)
         rcopy(attsend.at[at(p * T, T)], att.at[:, at(p * HD, HD)], att_ss.at[p], att_rs.at[p], {"ctx": p}).wait_recv()
 
-    loop(1, nctx, wait_att)
+    each(1, nctx, wait_att)
     mark("norm_dispatch")
     summed = residual[...].astype(F32) + att[...].astype(F32)
     summed_s[...] = summed
@@ -421,7 +432,8 @@
         probs_t[at(p * L, L), :] = probs
         probs_h[:, at(p * T, T)] = probs.astype(BF16)
 
-    loop(0, nctx, back_probs)
+    loop(0, nctx, back_probs, BATCH)
+    kh_t[...] = jnp.transpose(kh[...])
     mark("forward_grads")
     for g in range(GROUPS):
         near_forward(0, rows_g, g)
@@ -604,7 +616,7 @@
                     {"lang": to},
                 ).start()
 
-            loop(max(1, g * LG), (g + 1) * LG, one)
+            each(max(1, g * LG), (g + 1) * LG, one)
         msg_r[phase, at(me * MR, MR), :] = msg_s[phase, 0:MR, :]
 
     def combine(phase):
@@ -652,7 +664,7 @@
     def gr_copy(to, owner, sem_at):
         return rcopy(grsend.at[:, at(to * HD, HD)], grh.at[at(owner * T, T)], gr_ss.at[sem_at], gr_rs.at[owner], {"ctx": to})
 
-    loop(1, nctx, lambda i: gr_copy((c + i) % nctx, c, (c + i) % nctx).start())
+    each(1, nctx, lambda i: gr_copy(lax.rem(c + i, nctx), c, lax.rem(c + i, nctx)).start())
     grh[at(c * T, T), :] = grsend[:, at(c * HD, HD)]
     grad_res[...] = grsend[...]
     gain_part = jnp.sum(grad_normin * normed, axis=0, keepdims=True)
@@ -662,7 +674,7 @@
     def gain_copy(to, owner):
         return rcopy(gain_s, gain_c.at[owner], gain_ss.at[to], gain_rs.at[owner], {"ctx": to})
 
-    loop(1, nctx, lambda i: gain_copy((c + i) % nctx, c).start())
+    each(1, nctx, lambda i: gain_copy(lax.rem(c + i, nctx), c).start())
     gain_c[c] = gain_s[...]
 
     mark("return_ffn")
@@ -672,38 +684,38 @@
     def go_copy(n, src, dst, to, owner):
         return rcopy(src.at[at(to * T, T)], dst.at[:, at(owner * HD, HD)], go_ss.at[n, to], go_rs.at[n, owner], {"ctx": to})
 
-    loop(1, nctx, lambda i: gr_copy((c + i) % nctx, (c + i) % nctx, (c + i) % nctx).wait_recv())
+    each(1, nctx, lambda i: gr_copy(lax.rem(c + i, nctx), lax.rem(c + i, nctx), lax.rem(c + i, nctx)).wait_recv())
     mark("grad_values")
     gvsend[...] = dot_nn(probs_h[...], grh[...]).astype(BF16)
-    loop(1, nctx, lambda i: go_copy(2, gvsend, gv_hbm, (c + i) % nctx, c).start())
+    each(1, nctx, lambda i: go_copy(2, gvsend, gv_hbm, lax.rem(c + i, nctx), c).start())
     mark("gain")
 
-    loop(1, nctx, lambda i: gain_copy((c + i) % nctx, (c + i) % nctx).wait_recv())
+    each(1, nctx, lambda i: gain_copy(lax.rem(c + i, nctx), lax.rem(c + i, nctx)).wait_recv())
     gain_l_s[...] = jnp.sum(gain_c[...], axis=0)
 
     def gainl_copy(to, owner):
         return rcopy(gain_l_s, gain_l.at[owner], gainl_ss.at[to], gainl_rs.at[owner], {"lang": to})
 
-    loop(1, nlang, lambda i: gainl_copy((me + i) % nlang, me).start())
+    each(1, nlang, lambda i: gainl_copy(lax.rem(me + i, nlang), me).start())
     gain_l[me] = gain_l_s[...]
     mark("backward_loop")
 
     def backward(i):
-        p = (c + 1 + i) % nctx
+        p = lax.rem(c + 1 + i, nctx)
         probs = probs_t[at(p * L, L), :]
         gp = dot_nt(vh[...], grh[at(p * T, T), :])
         gs = (probs * (gp - jnp.sum(probs * gp, axis=0, keepdims=True))).astype(BF16)
         probs_h[:, at(p * T, T)] = gs
-        gqsend[at(p * T, T), :] = (dot_nn(jnp.transpose(gs), kh[...]) * scale).astype(BF16)
+        gqsend[at(p * T, T), :] = jnp.transpose(dot_nn(kh_t[...], gs) * scale).astype(BF16)
 
         @pl.when(i < nctx - 1)
         def _():
             go_copy(0, gqsend, gq_hbm, p, c).start()
 
-    loop(0, nctx, backward)
+    loop(0, nctx, backward, BATCH)
     mark("send_keys")
     gksend[...] = (dot_nn(probs_h[...], qh[...]) * scale).astype(BF16)
-    loop(1, nctx, lambda i: go_copy(1, gksend, gk_hbm, (c + i) % nctx, c).start())
+    each(1, nctx, lambda i: go_copy(1, gksend, gk_hbm, lax.rem(c + i, nctx), c).start())
     triples = ((gqsend, gq_hbm), (gksend, gk_hbm), (gvsend, gv_hbm))
     own_out = [
         pltpu.make_async_copy(src.at[at(c * T, T)], dst.at[:, at(c * HD, HD)], loc_sem.at[3 + n])
@@ -717,27 +729,20 @@
     layer_out[...] = (summed_s[...] + gn_s[...]).astype(BF16)
 
     mark("gain_wait")
-    loop(1, nlang, lambda i: gainl_copy((me + i) % nlang, (me + i) % nlang).wait_recv())
+    each(1, nlang, lambda i: gainl_copy(lax.rem(me + i, nlang), lax.rem(me + i, nlang)).wait_recv())
     grad_gain[...] = jnp.sum(gain_l[...], axis=0)
 
     mark("wait_out")
-    def wait_out(i):
-        p = (c + i) % nctx
-        for n, (src, dst) in enumerate(triples):
-            go_copy(n, src, dst, p, p).wait_recv()
-
-    loop(1, nctx, wait_out)
-
     mark("wait_sent")
     def sent_ctx(i):
-        p = (c + i) % nctx
+        p = lax.rem(c + i, nctx)
         for n in range(4):
             in_copy(n, p, c).wait_send()
         rcopy(attsend.at[at(p * T, T)], att.at[:, at(c * HD, HD)], att_ss.at[p], att_rs.at[c], {"ctx": p}).wait_send()
         gr_copy(p, c, p).wait_send()
         gain_copy(p, c).wait_send()
-        for n, (src, dst) in enumerate(triples):
-            go_copy(n, src, dst, p, c).wait_send()
+        for n in (0, 2):
+            go_copy(n, triples[n][0], triples[n][1], p, c).wait_send()
 
     loop(1, nctx, sent_ctx)
 
@@ -748,9 +753,9 @@
                 msg_r.at[phase, at(d * MR, MR)],
                 lang_ss.at[phase, d],
                 lang_rs.at[phase, d],
-                {"lang": (me + d) % nlang},
+                {"lang": lax.rem(me + d, nlang)},
             ).wait_send()
-        gainl_copy((me + d) % nlang, me).wait_send()
+        gainl_copy(lax.rem(me + d, nlang), me).wait_send()
 
     loop(1, nlang, sent_lang)
 
@@ -775,6 +780,14 @@
         copy.wait()
     for copy in out_w:
         copy.wait()
+    def wait_out(i):
+        p = lax.rem(c + i, nctx)
+        for n, (src, dst) in enumerate(triples):
+            go_copy(n, src, dst, p, p).wait_recv()
+
+    each(1, nctx, wait_out)
+
+    each(1, nctx, lambda i: go_copy(1, gksend, gk_hbm, lax.rem(c + i, nctx), c).wait_send())
     mark(None)
 
 
@@ -830,6 +843,7 @@
         vmem32(L, T),
         vmem32(nctx * L, T),
         vmem(L, L),
+        vmem(HD, L),
         vmem(L, HD),
         vmem(T, D),
         vmem(D, F),
@@ -918,7 +932,7 @@
         in_specs=[anywhere] * 3 + [inside] * 6 + [anywhere] * 3,
         out_specs=(inside, anywhere, anywhere, anywhere, inside, inside, anywhere, anywhere, anywhere),
         scratch_shapes=scratch,
-        compiler_params=pltpu.CompilerParams(collective_id=0, has_side_effects=True, vmem_limit_bytes=58 * 1024 * 1024),
+        compiler_params=pltpu.CompilerParams(collective_id=0, has_side_effects=True, vmem_limit_bytes=62 * 1024 * 1024),
         cost_estimate=pl.CostEstimate(flops=16_000_000_000, bytes_accessed=10_000_000, transcendentals=3_000_000),
         name="layer",
     )(

time: 117 us -> 114 us (0.974)
  Pallas kernels: 116 us -> 113 us
    pallas_call x1, Pallas kernels: 112 us -> 109 us  [local(): pl.pallas_call(functools.partial(kernel, nctx, nlang), out_shape=(shape(T...]
where the time goes in v1:
time: 114 us
  Pallas kernels  113 us (99%)
    pallas_call x1, Pallas kernels, local(): pl.pallas_call(functools.partial(kernel, nctx, nlang), out_shape=(shape(T...  109 us
    pallas_call x1, Pallas kernels, local(): pl.pallas_call(store, out_shape=tuple((jax.ShapeDtypeStruct(o.shape, o.dt...  4.3 us

profile of v1, /device:TPU:1, one launch (start us, length us, event | category | flops | bytes accessed | tf_op | source)
XLA Modules:
  0.0 113.8 jit_solution(9764087625160391818)
XLA Ops:
  0.6 108.6 %layer.1 = (bf16[128,1024]{1,0:T(8,128)(2,1)}, bf16[128,1024]{1,0:T(8,128)(2,1)}, bf16[128,1024]{1,0:T(8,128)(2,1)}, bf16[128,1024]{1,0:T(8,128)(2,1)}, bf16[128...) custom-call(bf16[128,1024]{1,0:T(8,128)(2,1)} %bitcast.26, ...), custom_call_target="tpu_custom_call" | custom-call | flops 16000000000 | bytes 10000000 | tf_op jit(solution)/shard_map/layer/pallas_call | solution.py:919
  109.3 4.3 %store.1 = (bf16[128,1024]{1,0:T(8,128)(2,1)}, bf16[128,1024]{1,0:T(8,128)(2,1)}, bf16[128,1024]{1,0:T(8,128)(2,1)}, bf16[128,1024]{1,0:T(8,128)(2,1)}, bf16[128...) custom-call(bf16[128,1024]{1,0:T(8,128)(2,1)} %get-tuple-element.27., ...), custom_call_target="tpu_custom_call" | custom-call | tf_op jit(solution)/shard_map/store/pallas_call | solution.py:952

commit v2 on v1

--- a/solution.py
+++ b/solution.py
@@ -437,22 +437,22 @@
     mark("forward_grads")
     for g in range(GROUPS):
         near_forward(0, rows_g, g)
-    mark("norm_rows")
-    for g in range(GROUPS):
-        gather_send(1, rows_n, 1, g)
-        half_forward(0, rows_g, g)
     mark("grad_hidden")
     weight_in[0].wait()
     CR = GROUPS * 2 * RG
     for g in range(GROUPS):
-        for what in range(5):
+        for what in range(3):
             sib_wait(0, rows_g, g, what)
 
     def grad_hidden(i):
-        rows = at(i * CR, CR, 16)
+        rows = at((x + i + i // 2 - 2 * (i // 3)) % X * CR, CR, 16)
         gh_s[rows, :] = dot_nt(rows_g[rows, :], wd[...])
 
-    loop(0, X, grad_hidden)
+    loop(0, X - 1, grad_hidden)
+    mark("norm_rows")
+    for g in range(GROUPS):
+        gather_send(1, rows_n, 1, g)
+        half_forward(0, rows_g, g)
     weight_in[1].wait()
     weight_in[2].wait()
 
@@ -558,6 +558,10 @@
             sum_near(0, g, side)
     for g in range(GROUPS):
         half_forward(1, rows_n, g)
+    for g in range(GROUPS):
+        for what in (3, 4):
+            sib_wait(0, rows_g, g, what)
+    loop(X - 1, X, grad_hidden)
     mark("feed_across")
 
     def feed_across(g):
@@ -647,8 +651,8 @@
     ]
     out_w[0].start()
     out_w[1].start()
-    loop(0, F // FT, grad_wd)
-    out_w[2].start()
+    wd_half = F // FT // 2
+    loop(0, wd_half, grad_wd)
 
     mark("combine_grads")
     combine(2)
@@ -679,6 +683,8 @@
 
     mark("return_ffn")
     return_send(1, 3)
+    loop(wd_half, F // FT, grad_wd)
+    out_w[2].start()
 
     mark("backward")
     def go_copy(n, src, dst, to, owner):

time: 114 us -> 114 us (level)
  no operation moved by 1% of the time
where the time goes in v2:
time: 114 us; the launch traced here: 113 us
  Pallas kernels  113 us (99%)
    pallas_call x1, Pallas kernels, local(): pl.pallas_call(functools.partial(kernel, nctx, nlang), out_shape=(shape(T...  108 us
    pallas_call x1, Pallas kernels, local(): pl.pallas_call(store, out_shape=tuple((jax.ShapeDtypeStruct(o.shape, o.dt...  4.3 us

profile of v2, /device:TPU:1, one launch (start us, length us, event | category | flops | bytes accessed | tf_op | source)
XLA Modules:
  0.0 113.4 jit_solution(17686722903598642897)
XLA Ops:
  0.6 108.3 %layer.1 = (bf16[128,1024]{1,0:T(8,128)(2,1)}, bf16[128,1024]{1,0:T(8,128)(2,1)}, bf16[128,1024]{1,0:T(8,128)(2,1)}, bf16[128,1024]{1,0:T(8,128)(2,1)}, bf16[128...) custom-call(bf16[128,1024]{1,0:T(8,128)(2,1)} %bitcast.26, ...), custom_call_target="tpu_custom_call" | custom-call | flops 16000000000 | bytes 10000000 | tf_op jit(solution)/shard_map/layer/pallas_call | solution.py:925
  108.9 4.3 %store.1 = (bf16[128,1024]{1,0:T(8,128)(2,1)}, bf16[128,1024]{1,0:T(8,128)(2,1)}, bf16[128,1024]{1,0:T(8,128)(2,1)}, bf16[128,1024]{1,0:T(8,128)(2,1)}, bf16[128...) custom-call(bf16[128,1024]{1,0:T(8,128)(2,1)} %get-tuple-element.27., ...), custom_call_target="tpu_custom_call" | custom-call | tf_op jit(solution)/shard_map/store/pallas_call | solution.py:958
